TPU v7x, 256 devices: a whole 4x4x8 slice. The times are simulated.
256 devices in a mesh: gx: 32 (over z_lo, y, core), gy: 8 (over x, z_hi).
Axes of the slice: x: 4, y: 4, z: 8 (z_hi: 2, z_lo: 4; z = z_hi * 4 + z_lo), core: 2. Of those that a mesh axis runs over, the one named last changes fastest.
Arguments:
- features: bfloat16 [512, 512, 128], P(('gx', 'gy')), may hold values from -6 to 6
- occupied: int32 [512, 512], P(('gx', 'gy')), may hold values 0 or 1
- weight_one: bfloat16 [27, 128, 128], replicated, may hold values from -0.109375 to 0.109375
- bias_one: float32 [128], replicated, may hold values from -3 to 3
- weight_two: bfloat16 [27, 128, 128], replicated, may hold values from -0.109375 to 0.109375
- cotangent: bfloat16 [512, 512, 128], P(('gx', 'gy')), may hold values from -6 to 6
- neighbours: int32 [512, 27], P(('gx', 'gy')), may hold values from 0 to 18, as said below
- send_x: int32 [256, 2, 6], P(('gx', 'gy')), may hold values from 0 to 18, as said below
- send_y: int32 [256, 2, 2], P(('gx', 'gy')), may hold values from 0 to 18, as said below
Outputs:
- output: bfloat16 [512, 512, 128], P(('gx', 'gy'))
- grad_features: bfloat16 [512, 512, 128], P(('gx', 'gy'))
- grad_weight_one: float32 [27, 128, 128], replicated
- grad_weight_two: float32 [27, 128, 128], replicated
Inputs may be any that keep to these rules, and one draw needn't show every extreme that they name: `neighbours`: each tile is 2 x 2 x 2 bricks of the map, tiles laid out with x over gx and y over gy. A tile's live bricks fill its first slots, and some tile is full in every draw. A live brick's entry k names the pool row holding the brick at brick offset (k // 9 - 1, k // 3 % 3 - 1, k % 3 - 1), or 18 where that brick is empty or lies outside the map; entry 13 names its own slot; a dead slot's entries are all 18. The lists describe one map, so neighbourhood is symmetric. send_y[t, 0] lists in slot order the live slots of tile t in its top layer of bricks along y, send_y[t, 1] those in its bottom layer; the rest is 18. send_x[t, 0] lists in row order the pool rows below 6 of tile t (its own bricks and those it received along y) whose bricks lie in its top layer along x, send_x[t, 1] those in its bottom layer; the rest is 18.
All inputs are finite; a program needn't handle non-finite values. No bound on the sum of `occupied` on one device may be relied on, other than what follows from the above.
Results may differ from a plain program's by a relative error of at most 0.015.
Values may be sent and summed in bfloat16 or wider, within the bound.
A program may use at most 128 MiB of HBM per device.

v0:
```python
import math
import jax
import jax.numpy as jnp
from jax import lax
from jax.sharding import PartitionSpec as P

EDGE = 8
KVOL = 27


def shifted(block, axis, distance):
    devices = range(lax.axis_size(axis))
    route = [(i - distance, i) for i in devices if i - distance in devices]
    return lax.ppermute(block, axis, route)


def cut_layer(portion, side_code, along_axis):
    extent = portion.shape[along_axis]
    if side_code == 0:
        return lax.slice_in_dim(portion, extent - 1, extent, axis=along_axis)
    if side_code == 2:
        return lax.slice_in_dim(portion, 0, 1, axis=along_axis)
    return portion


def pick_rows(bricks, row_index):
    row_count = bricks.shape[0]
    clipped = jnp.where(row_index < row_count, row_index, row_count)
    padded_rows = jnp.concatenate([bricks, jnp.zeros((1,) + bricks.shape[1:], bricks.dtype)], 0)
    return padded_rows[clipped]


def fill_pool(voxel_field, send_x, send_y, brick_edge):
    slots, voxels, channels = voxel_field.shape
    bricks = voxel_field.reshape(slots, brick_edge, brick_edge, brick_edge, channels)
    gathered = [bricks]
    for lane_idx, shift_by, side_code in ((0, 1, 0), (1, -1, 2)):
        chosen = pick_rows(bricks, send_y[0, lane_idx])
        arrived = shifted(chosen, "gy", shift_by)
        gathered.append(arrived)
    first_section = jnp.concatenate(gathered, 0)
    pooled = [first_section]
    for lane_idx, shift_by, side_code in ((0, 1, 0), (1, -1, 2)):
        chosen = pick_rows(first_section, send_x[0, lane_idx])
        arrived = shifted(chosen, "gx", shift_by)
        pooled.append(arrived)
    pooled.append(jnp.zeros((1,) + bricks.shape[1:], bricks.dtype))
    return jnp.concatenate(pooled, 0)


def gather_block(pool_rows, neighbours):
    layers_x = []
    for off_x in range(3):
        layers_y = []
        for off_y in range(3):
            layers_z = []
            for off_z in range(3):
                portion = cut_layer(cut_layer(cut_layer(pool_rows, off_x, 1), off_y, 2), off_z, 3)
                layers_z.append(portion[neighbours[:, 9 * off_x + 3 * off_y + off_z]])
            layers_y.append(jnp.concatenate(layers_z, axis=3))
        layers_x.append(jnp.concatenate(layers_y, axis=2))
    return jnp.concatenate(layers_x, axis=1)


def to_columns(padded_block, brick_edge):
    tap_list = []
    for off_x in range(3):
        for off_y in range(3):
            for off_z in range(3):
                tap_list.append(
                    padded_block[
                        :,
                        off_x : off_x + brick_edge,
                        off_y : off_y + brick_edge,
                        off_z : off_z + brick_edge,
                    ]
                )
    stacked = jnp.stack(tap_list, axis=4)
    return stacked.reshape(-1, len(tap_list) * padded_block.shape[-1])


def transpose_conv(grad_field, weight, neighbours, send_x, send_y, brick_edge):
    slots, voxels, channels = grad_field.shape
    flipped = jnp.flip(weight, 0).transpose(0, 2, 1).reshape(-1, channels)
    pool_rows = fill_pool(grad_field, send_x, send_y, brick_edge)
    columns = to_columns(gather_block(pool_rows, neighbours), brick_edge)
    result = jnp.dot(columns, flipped, preferred_element_type=jnp.float32)
    return result.reshape(slots, voxels, channels)


def on_device(
    features, occupied, weight_one, bias_one, weight_two, cotangent, neighbours, send_x, send_y
):
    slots, voxels, channels = features.shape
    brick_edge = EDGE
    pool_end = slots + 2 * send_y.shape[2] + 2 * send_x.shape[2]
    live_bricks = (neighbours[:, 13] != pool_end).astype(jnp.int32)
    voxel_mask = (occupied * live_bricks[:, None]).astype(jnp.float32)[:, :, None]
    mask_half = voxel_mask.astype(jnp.bfloat16)
    masked = features * mask_half
    flat_one = weight_one.reshape(KVOL * channels, channels)
    flat_two = weight_two.reshape(KVOL * channels, channels)
    cols_input = to_columns(
        gather_block(fill_pool(masked, send_x, send_y, brick_edge), neighbours), brick_edge
    )
    preact = (
        jnp.dot(cols_input, flat_one, preferred_element_type=jnp.float32).reshape(
            slots, voxels, channels
        )
        + bias_one
    )
    hidden = (jax.nn.relu(preact) * voxel_mask).astype(jnp.bfloat16)
    cols_hidden = to_columns(
        gather_block(fill_pool(hidden, send_x, send_y, brick_edge), neighbours), brick_edge
    )
    second_conv = jnp.dot(cols_hidden, flat_two, preferred_element_type=jnp.float32).reshape(
        slots, voxels, channels
    )
    output = (second_conv * voxel_mask + masked.astype(jnp.float32)).astype(jnp.bfloat16)
    grad_out = cotangent * mask_half
    back_two = transpose_conv(grad_out, weight_two, neighbours, send_x, send_y, brick_edge)
    contract = (((0,), (0,)), ((), ()))
    sum_two = lax.dot_general(
        cols_hidden,
        grad_out.reshape(slots * voxels, channels),
        contract,
        preferred_element_type=jnp.float32,
    )
    grad_hidden = jnp.where(preact > 0, back_two * voxel_mask, 0.0).astype(jnp.bfloat16)
    back_one = transpose_conv(grad_hidden, weight_one, neighbours, send_x, send_y, brick_edge)
    sum_one = lax.dot_general(
        cols_input,
        grad_hidden.reshape(slots * voxels, channels),
        contract,
        preferred_element_type=jnp.float32,
    )
    sum_one, sum_two = lax.psum((sum_one, sum_two), ("gx", "gy"))
    grad_scale = 1.0 / math.sqrt(slots * voxels * lax.axis_size("gx") * lax.axis_size("gy"))
    grad_features = ((cotangent.astype(jnp.float32) + back_one) * voxel_mask).astype(jnp.bfloat16)
    grad_weight_one = (sum_one * grad_scale).reshape(KVOL, channels, channels)
    grad_weight_two = (sum_two * grad_scale).reshape(KVOL, channels, channels)
    return (output, grad_features, grad_weight_one, grad_weight_two)


def solution(mesh):
    in_specs = (
        P(("gx", "gy"), None, None),
        P(("gx", "gy"), None),
        P(),
        P(),
        P(),
        P(("gx", "gy"), None, None),
        P(("gx", "gy"), None),
        P(("gx", "gy"), None, None),
        P(("gx", "gy"), None, None),
    )
    out_specs = (P(("gx", "gy"), None, None), P(("gx", "gy"), None, None), P(), P())
    return jax.shard_map(
        on_device, mesh=mesh, in_specs=in_specs, out_specs=out_specs, check_vma=False
    )
```

profile of v0, /device:TPU:2, one launch (start us, length us, event | category | flops | bytes accessed | tf_op | source)
XLA Modules:
  0.0 849.3 jit_solution(8771616513204699121)
XLA Ops:
  13.2 9.1 %collective-permute-start = (bf16[2,8,8,8,128]{4,3,2,1,0:T(8,128)(2,1)}, bf16[2,8,8,8,128]{4,3,2,1,0:T(8,128)(2,1)S(1)}, u32[]{:S(2)}, u32[]{:S(2)}) collective-permute-start(bf16[2,8,8,8,128]{4,3,2,1,0:T(8,128)(2,1)} %gather_fusion), channel_id=1, source_target_pairs={{0,1},{1,2},{2,3},{3,4},{4,5},{5,6},{6,7},{8,9},{9,10},{10,11},{11... | collective-permute-start | bytes 786440 | tf_op jit(solution)/shard_map/ppermute | solution.py:14
  26.8 7.8 collective-permute-start.8
  52.4 8.5 collective-permute-done.8
  60.8 9.4 %collective-permute-done.9 = bf16[2,8,8,8,128]{4,3,2,1,0:T(8,128)(2,1)S(1)} collective-permute-done((bf16[2,8,8,8,128]{4,3,2,1,0:T(8,128)(2,1)}, bf16[2,8,8,8,128]{4,3,2,1,0:T(8,128)(2,1)S(1)}, u32[]{:S(2)}, u32[]{:S(2)}) %collective-permute-start.9) | collective-permute-done | bytes 262176 | tf_op jit(solution)/shard_map/ppermute | solution.py:14
  82.2 4.0 collective-permute-start.10
  257.5 4.1 copy.248
  283.6 4.7 copy.198
  288.4 4.6 multiply_convert_fusion
  301.1 6.5 collective-permute-start.12
  307.6 4.1 collective-permute-start.13
  311.7 5.6 collective-permute-start.4
  317.4 5.0 collective-permute-start.5
  325.2 20.1 %collective-permute-done.13 = bf16[2,8,8,8,128]{4,3,2,1,0:T(8,128)(2,1)S(1)} collective-permute-done((bf16[2,8,8,8,128]{4,3,2,1,0:T(8,128)(2,1)}, bf16[2,8,8,8,128]{4,3,2,1,0:T(8,128)(2,1)S(1)}, u32[]{:S(2)}, u32[]{:S(2)}) %collective-permute-start.13) | collective-permute-done | bytes 262176 | tf_op jit(solution)/shard_map/ppermute | solution.py:14
  345.4 11.2 %collective-permute-done.5 = bf16[2,8,8,8,128]{4,3,2,1,0:T(8,128)(2,1)} collective-permute-done((bf16[2,8,8,8,128]{4,3,2,1,0:T(8,128)(2,1)}, bf16[2,8,8,8,128]{4,3,2,1,0:T(8,128)(2,1)}, u32[]{:S(2)}, u32[]{:S(2)}) %collective-permute-start.5) | collective-permute-done | bytes 262176 | tf_op jit(solution)/shard_map/ppermute | solution.py:14
  359.5 2.9 collective-permute-start.6
  362.4 6.3 fusion.65
  376.6 3.1 collective-permute-start.14
  404.0 4.9 fusion.58
  557.5 4.2 copy.223
  564.6 3.3 fusion.66
  570.2 4.7 copy.274
  575.0 4.0 fusion.5
  581.7 256.3 %all-reduce.7.cloned.1.call-done = (f32[3456,128]{1,0:T(8,128)}, f32[3456,128]{1,0:T(8,128)}) async-done(((f32[3456,128]{1,0:T(8,128)}, f32[3456,128]{1,0:T(8,128)}), (f32[3456,128]{1,0:T(8,128)}, f32[3456,128]{1,0:T(8,128)})) %all-reduce.7.cloned.1.call-update) | async-done | bytes 3538960 | tf_op jit(solution)/shard_map/psum | solution.py:137
  838.0 2.9 broadcast_multiply_fusion.1
  (737 shorter events, 435.6 us)
Async XLA Ops:
  7.2 830.8 %all-reduce.7.cloned.1.call-start = ((), (), s32[]{:S(2)}) async-start(), calls=%async_computation | async-start | bytes 7077888 | tf_op jit(solution)/shard_map/psum | solution.py:137
  11.8 58.5 %copy-start.6 = (bf16[2,512,128]{2,1,0:T(8,128)(2,1)}, bf16[2,512,128]{2,1,0:T(8,128)(2,1)S(1)}, u32[]{:S(2)}) copy-start(bf16[2,512,128]{2,1,0:T(8,128)(2,1)S(1)} %get-tuple-element.125) | copy-start | bytes 786436
  13.2 39.2 %collective-permute-start = (bf16[2,8,8,8,128]{4,3,2,1,0:T(8,128)(2,1)}, bf16[2,8,8,8,128]{4,3,2,1,0:T(8,128)(2,1)S(1)}, u32[]{:S(2)}, u32[]{:S(2)}) collective-permute-start(bf16[2,8,8,8,128]{4,3,2,1,0:T(8,128)(2,1)} %gather_fusion), channel_id=1, source_target_pairs={{0,1},{1,2},{2,3},{3,4},{4,5},{5,6},{6,7},{8,9},{9,10},{10,11},{11... | collective-permute-start | bytes 786440 | tf_op jit(solution)/shard_map/ppermute | solution.py:14
  23.6 28.8 %collective-permute-start.1 = (bf16[2,8,8,8,128]{4,3,2,1,0:T(8,128)(2,1)}, bf16[2,8,8,8,128]{4,3,2,1,0:T(8,128)(2,1)S(1)}, u32[]{:S(2)}, u32[]{:S(2)}) collective-permute-start(bf16[2,8,8,8,128]{4,3,2,1,0:T(8,128)(2,1)} %gather_fusion.1), channel_id=1, source_target_pairs={{1,0},{2,1},{3,2},{4,3},{5,4},{6,5},{7,6},{9,8},{10,9},{11,10},{12... | collective-permute-start | bytes 786440 | tf_op jit(solution)/shard_map/ppermute | solution.py:14
  26.8 34.0 %collective-permute-start.8 = (bf16[2,8,8,8,128]{4,3,2,1,0:T(8,128)(2,1)}, bf16[2,8,8,8,128]{4,3,2,1,0:T(8,128)(2,1)S(1)}, u32[]{:S(2)}, u32[]{:S(2)}) collective-permute-start(bf16[2,8,8,8,128]{4,3,2,1,0:T(8,128)(2,1)} %gather_fusion.62), channel_id=1, source_target_pairs={{0,1},{1,2},{2,3},{3,4},{4,5},{5,6},{6,7},{8,9},{9,10},{10,11},{11... | collective-permute-start | bytes 786440 | tf_op jit(solution)/shard_map/ppermute | solution.py:14
  35.9 34.3 %collective-permute-start.9 = (bf16[2,8,8,8,128]{4,3,2,1,0:T(8,128)(2,1)}, bf16[2,8,8,8,128]{4,3,2,1,0:T(8,128)(2,1)S(1)}, u32[]{:S(2)}, u32[]{:S(2)}) collective-permute-start(bf16[2,8,8,8,128]{4,3,2,1,0:T(8,128)(2,1)} %gather_fusion.63), channel_id=1, source_target_pairs={{1,0},{2,1},{3,2},{4,3},{5,4},{6,5},{7,6},{9,8},{10,9},{11,10},{12... | collective-permute-start | bytes 786440 | tf_op jit(solution)/shard_map/ppermute | solution.py:14
  44.0 106.9 %copy-start.65 = (s32[1024]{0:T(1024)}, s32[1024]{0:T(1024)S(1)}, u32[]{:S(2)}) copy-start(s32[1024]{0:T(1024)S(1)} %get-tuple-element.180) | copy-start | bytes 12292
  72.5 18.1 %collective-permute-start.2 = (bf16[6,8,8,8,128]{4,3,2,1,0:T(8,128)(2,1)}, bf16[6,8,8,8,128]{4,3,2,1,0:T(8,128)(2,1)}, u32[]{:S(2)}, u32[]{:S(2)}) collective-permute-start(bf16[6,8,8,8,128]{4,3,2,1,0:T(8,128)(2,1)} %gather_fusion.2), channel_id=1, source_target_pairs={{0,8},{8,16},{16,24},{24,32},{32,40},{40,48},{48,56},{56,64},{64,7... | collective-permute-start | bytes 2359304 | tf_op jit(solution)/shard_map/ppermute | solution.py:14
  76.3 16.4 %collective-permute-start.3 = (bf16[6,8,8,8,128]{4,3,2,1,0:T(8,128)(2,1)}, bf16[6,8,8,8,128]{4,3,2,1,0:T(8,128)(2,1)S(1)}, u32[]{:S(2)}, u32[]{:S(2)}) collective-permute-start(bf16[6,8,8,8,128]{4,3,2,1,0:T(8,128)(2,1)} %gather_fusion.3), channel_id=1, source_target_pairs={{8,0},{16,8},{24,16},{32,24},{40,32},{48,40},{56,48},{64,56},{72,6... | collective-permute-start | bytes 2359304 | tf_op jit(solution)/shard_map/ppermute | solution.py:14
  82.2 21.7 %collective-permute-start.10 = (bf16[6,8,8,8,128]{4,3,2,1,0:T(8,128)(2,1)}, bf16[6,8,8,8,128]{4,3,2,1,0:T(8,128)(2,1)S(1)}, u32[]{:S(2)}, u32[]{:S(2)}) collective-permute-start(bf16[6,8,8,8,128]{4,3,2,1,0:T(8,128)(2,1)} %gather_fusion.64), channel_id=1, source_target_pairs={{0,8},{8,16},{16,24},{24,32},{32,40},{40,48},{48,56},{56,64},{64,7... | collective-permute-start | bytes 2359304 | tf_op jit(solution)/shard_map/ppermute | solution.py:14
  86.2 22.1 %collective-permute-start.11 = (bf16[6,8,8,8,128]{4,3,2,1,0:T(8,128)(2,1)}, bf16[6,8,8,8,128]{4,3,2,1,0:T(8,128)(2,1)S(1)}, u32[]{:S(2)}, u32[]{:S(2)}) collective-permute-start(bf16[6,8,8,8,128]{4,3,2,1,0:T(8,128)(2,1)} %gather_fusion.65), channel_id=1, source_target_pairs={{8,0},{16,8},{24,16},{32,24},{40,32},{48,40},{56,48},{64,56},{72,6... | collective-permute-start | bytes 2359304 | tf_op jit(solution)/shard_map/ppermute | solution.py:14
  155.8 84.0 %copy-start.8 = (bf16[19,8,8,1,128]{4,3,2,1,0:T(2,128)(2,1)S(1)}, bf16[19,8,8,1,128]{4,3,2,1,0:T(2,128)(2,1)}, u32[]{:S(2)}) copy-start(bf16[19,8,8,1,128]{4,3,2,1,0:T(2,128)(2,1)} %get-tuple-element.58) | copy-start | bytes 933892
  298.1 58.6 %copy-start.18 = (bf16[1,8,8,8,128]{4,3,2,1,0:T(8,128)(2,1)S(1)}, bf16[1,8,8,8,128]{4,3,2,1,0:T(8,128)(2,1)}, u32[]{:S(2)}) copy-start(bf16[1,8,8,8,128]{4,3,2,1,0:T(8,128)(2,1)} %copy-done.17) | copy-start | bytes 393220
  301.1 24.1 %collective-permute-start.12 = (bf16[2,8,8,8,128]{4,3,2,1,0:T(8,128)(2,1)}, bf16[2,8,8,8,128]{4,3,2,1,0:T(8,128)(2,1)S(1)}, u32[]{:S(2)}, u32[]{:S(2)}) collective-permute-start(bf16[2,8,8,8,128]{4,3,2,1,0:T(8,128)(2,1)} %gather_fusion.93), channel_id=1, source_target_pairs={{0,1},{1,2},{2,3},{3,4},{4,5},{5,6},{6,7},{8,9},{9,10},{10,11},{11... | collective-permute-start | bytes 786440 | tf_op jit(solution)/shard_map/ppermute | solution.py:14
  307.6 37.7 %collective-permute-start.13 = (bf16[2,8,8,8,128]{4,3,2,1,0:T(8,128)(2,1)}, bf16[2,8,8,8,128]{4,3,2,1,0:T(8,128)(2,1)S(1)}, u32[]{:S(2)}, u32[]{:S(2)}) collective-permute-start(bf16[2,8,8,8,128]{4,3,2,1,0:T(8,128)(2,1)} %gather_fusion.94), channel_id=1, source_target_pairs={{1,0},{2,1},{3,2},{4,3},{5,4},{6,5},{7,6},{9,8},{10,9},{11,10},{12... | collective-permute-start | bytes 786440 | tf_op jit(solution)/shard_map/ppermute | solution.py:14
  311.7 33.7 %collective-permute-start.4 = (bf16[2,8,8,8,128]{4,3,2,1,0:T(8,128)(2,1)}, bf16[2,8,8,8,128]{4,3,2,1,0:T(8,128)(2,1)S(1)}, u32[]{:S(2)}, u32[]{:S(2)}) collective-permute-start(bf16[2,8,8,8,128]{4,3,2,1,0:T(8,128)(2,1)} %gather_fusion.31), channel_id=1, source_target_pairs={{0,1},{1,2},{2,3},{3,4},{4,5},{5,6},{6,7},{8,9},{9,10},{10,11},{11... | collective-permute-start | bytes 786440 | tf_op jit(solution)/shard_map/ppermute | solution.py:14
  317.4 39.3 %collective-permute-start.5 = (bf16[2,8,8,8,128]{4,3,2,1,0:T(8,128)(2,1)}, bf16[2,8,8,8,128]{4,3,2,1,0:T(8,128)(2,1)}, u32[]{:S(2)}, u32[]{:S(2)}) collective-permute-start(bf16[2,8,8,8,128]{4,3,2,1,0:T(8,128)(2,1)} %gather_fusion.32), channel_id=1, source_target_pairs={{1,0},{2,1},{3,2},{4,3},{5,4},{6,5},{7,6},{9,8},{10,9},{11,10},{12... | collective-permute-start | bytes 786440 | tf_op jit(solution)/shard_map/ppermute | solution.py:14
  359.5 25.5 %collective-permute-start.6 = (bf16[6,8,8,8,128]{4,3,2,1,0:T(8,128)(2,1)}, bf16[6,8,8,8,128]{4,3,2,1,0:T(8,128)(2,1)}, u32[]{:S(2)}, u32[]{:S(2)}) collective-permute-start(bf16[6,8,8,8,128]{4,3,2,1,0:T(8,128)(2,1)} %gather_fusion.33), channel_id=1, source_target_pairs={{0,8},{8,16},{16,24},{24,32},{32,40},{40,48},{48,56},{56,64},{64,7... | collective-permute-start | bytes 2359304 | tf_op jit(solution)/shard_map/ppermute | solution.py:14
  370.3 16.7 %collective-permute-start.7 = (bf16[6,8,8,8,128]{4,3,2,1,0:T(8,128)(2,1)}, bf16[6,8,8,8,128]{4,3,2,1,0:T(8,128)(2,1)}, u32[]{:S(2)}, u32[]{:S(2)}) collective-permute-start(bf16[6,8,8,8,128]{4,3,2,1,0:T(8,128)(2,1)} %gather_fusion.34), channel_id=1, source_target_pairs={{8,0},{16,8},{24,16},{32,24},{40,32},{48,40},{56,48},{64,56},{72,6... | collective-permute-start | bytes 2359304 | tf_op jit(solution)/shard_map/ppermute | solution.py:14
  376.6 22.9 %collective-permute-start.14 = (bf16[6,8,8,8,128]{4,3,2,1,0:T(8,128)(2,1)}, bf16[6,8,8,8,128]{4,3,2,1,0:T(8,128)(2,1)S(1)}, u32[]{:S(2)}, u32[]{:S(2)}) collective-permute-start(bf16[6,8,8,8,128]{4,3,2,1,0:T(8,128)(2,1)} %gather_fusion.95), channel_id=1, source_target_pairs={{0,8},{8,16},{16,24},{24,32},{32,40},{40,48},{48,56},{56,64},{64,7... | collective-permute-start | bytes 2359304 | tf_op jit(solution)/shard_map/ppermute | solution.py:14
  379.6 29.3 %collective-permute-start.15 = (bf16[6,8,8,8,128]{4,3,2,1,0:T(8,128)(2,1)}, bf16[6,8,8,8,128]{4,3,2,1,0:T(8,128)(2,1)}, u32[]{:S(2)}, u32[]{:S(2)}) collective-permute-start(bf16[6,8,8,8,128]{4,3,2,1,0:T(8,128)(2,1)} %gather_fusion.96), channel_id=1, source_target_pairs={{8,0},{16,8},{24,16},{32,24},{40,32},{48,40},{56,48},{64,56},{72,6... | collective-permute-start | bytes 2359304 | tf_op jit(solution)/shard_map/ppermute | solution.py:14
  418.5 39.6 %copy-start.10 = (bf16[19,8,8,1,128]{4,3,2,1,0:T(2,128)(2,1)S(1)}, bf16[19,8,8,1,128]{4,3,2,1,0:T(2,128)(2,1)}, u32[]{:S(2)}) copy-start(bf16[19,8,8,1,128]{4,3,2,1,0:T(2,128)(2,1)} %get-tuple-element.85) | copy-start | bytes 933892
  458.9 58.8 %copy-start.13 = (bf16[2,8,8,1,128]{4,3,2,1,0:T(2,128)(2,1)}, bf16[2,8,8,1,128]{4,3,2,1,0:T(2,128)(2,1)S(1)}, u32[]{:S(2)}) copy-start(bf16[2,8,8,1,128]{4,3,2,1,0:T(2,128)(2,1)S(1)} %copy.209) | copy-start | bytes 98308
  459.1 65.7 %copy-start.9 = (bf16[19,8,8,1,128]{4,3,2,1,0:T(2,128)(2,1)S(1)}, bf16[19,8,8,1,128]{4,3,2,1,0:T(2,128)(2,1)}, u32[]{:S(2)}) copy-start(bf16[19,8,8,1,128]{4,3,2,1,0:T(2,128)(2,1)} %get-tuple-element.33) | copy-start | bytes 933892
  (87 other events, 756.2 us)
Sparse Core Ops, SparseCore 0:
  568.0 270.0 all-reduce.6
where the time goes:
time: 861 us; the launch traced here: 849 us
  local copies, waits for them, and re-layouts  408 us (47%)
  waiting for transfers between devices  306 us (36%)
  starting transfers between devices  60.5 us (7%)
  other arithmetic  35.3 us (4%)
  matrix products  22.9 us (3%)
  between operations  16.4 us (2%)
    psum x1, waiting for transfers between devices, on_device(): sum_one, sum_two = lax.psum((sum_one, sum_two), ('gx', 'gy'))  256 us
    gather x180, local copies, waits for them, and re-layouts, gather_block(): layers_z.append(portion[neighbours[:, 9 * off_x + 3 * off_y + off_z]])  186 us
    unnamed x387, local copies, waits for them, and re-layouts  122 us
    ppermute x16, starting transfers between devices, shifted(): return lax.ppermute(block, axis, route)  60.5 us
    ppermute x16, waiting for transfers between devices, shifted(): return lax.ppermute(block, axis, route)  49.9 us
    slice x24, local copies, waits for them, and re-layouts, cut_layer(): return lax.slice_in_dim(portion, extent - 1, extent, axis=along_axis)  43.2 us
    gather x16, local copies, waits for them, and re-layouts, pick_rows(): return padded_rows[clipped]  24.3 us
    another operation x8, local copies, waits for them, and re-layouts, to_columns(): stacked = jnp.stack(tap_list, axis=4)  20.3 us
  transfers between devices with their start and end apart: 17, of which 7 were waited for; matrix products, arithmetic and copies ran while one was open for 12% of the time, Pallas kernels for 0%

commit v1 on v0

--- a/solution.py
+++ b/solution.py
@@ -134,7 +134,7 @@
         contract,
         preferred_element_type=jnp.float32,
     )
-    sum_one, sum_two = lax.psum((sum_one, sum_two), ("gx", "gy"))
+    sum_one, sum_two = lax.psum(lax.psum((sum_one, sum_two), "gx"), "gy")
     grad_scale = 1.0 / math.sqrt(slots * voxels * lax.axis_size("gx") * lax.axis_size("gy"))
     grad_features = ((cotangent.astype(jnp.float32) + back_one) * voxel_mask).astype(jnp.bfloat16)
     grad_weight_one = (sum_one * grad_scale).reshape(KVOL, channels, channels)

time: 861 us -> 1150 us (1.34)
  waiting for transfers between devices: 306 us -> 603 us
    psum x1 -> x2, waiting for transfers between devices: 256 us -> 553 us  [on_device(): sum_one, sum_two = lax.psum(lax.psum((sum_one, sum_two), 'gx'), 'gy')]
    gather x180, local copies, waits for them, and re-layouts: 186 us -> 170 us  [gather_block(): layers_z.append(portion[neighbours[:, 9 * off_x + 3 * off_y + off_z]])]
    unnamed x387 -> x383, local copies, waits for them, and re-layouts: 122 us -> 130 us
  transfers between devices with their start and end apart: 17 -> 18, of which waited for: 7 -> 8; matrix products, arithmetic and copies ran while one was open for 12% -> 11% of each run, Pallas kernels for 0% -> 0%
where the time goes in v1:
time: 1150 us; the launch traced here: 1140 us
  waiting for transfers between devices  603 us (52%)
  local copies, waits for them, and re-layouts  400 us (35%)
  starting transfers between devices  60.6 us (5%)
  other arithmetic  36.8 us (3%)
  matrix products  22.9 us (2%)
  between operations  16.2 us (1%)
    psum x2, waiting for transfers between devices, on_device(): sum_one, sum_two = lax.psum(lax.psum((sum_one, sum_two), 'gx'), 'gy')  553 us
    gather x180, local copies, waits for them, and re-layouts, gather_block(): layers_z.append(portion[neighbours[:, 9 * off_x + 3 * off_y + off_z]])  170 us
    unnamed x383, local copies, waits for them, and re-layouts  130 us
    ppermute x16, starting transfers between devices, shifted(): return lax.ppermute(block, axis, route)  60.5 us
    ppermute x16, waiting for transfers between devices, shifted(): return lax.ppermute(block, axis, route)  49.9 us
    slice x24, local copies, waits for them, and re-layouts, cut_layer(): return lax.slice_in_dim(portion, extent - 1, extent, axis=along_axis)  43.2 us
    gather x16, local copies, waits for them, and re-layouts, pick_rows(): return padded_rows[clipped]  24.2 us
  transfers between devices with their start and end apart: 18, of which 8 were waited for; matrix products, arithmetic and copies ran while one was open for 11% of the time, Pallas kernels for 0%

profile of v1, /device:TPU:2, one launch (start us, length us, event | category | flops | bytes accessed | tf_op | source)
XLA Modules:
  0.0 1139.4 jit_solution(6604949132598571599)
XLA Ops:
  13.2 9.1 collective-permute-start
  26.8 7.8 collective-permute-start.8
  52.4 8.5 collective-permute-done.8
  60.8 9.4 collective-permute-done.9
  82.2 4.0 collective-permute-start.10
  257.3 4.1 copy.248
  283.4 4.7 copy.198
  288.2 4.6 multiply_convert_fusion
  300.8 6.5 collective-permute-start.12
  307.4 4.1 collective-permute-start.13
  311.5 5.6 collective-permute-start.4
  317.1 5.0 collective-permute-start.5
  325.0 20.1 %collective-permute-done.13 = bf16[2,8,8,8,128]{4,3,2,1,0:T(8,128)(2,1)S(1)} collective-permute-done((bf16[2,8,8,8,128]{4,3,2,1,0:T(8,128)(2,1)}, bf16[2,8,8,8,128]{4,3,2,1,0:T(8,128)(2,1)S(1)}, u32[]{:S(2)}, u32[]{:S(2)}) %collective-permute-start.13) | collective-permute-done | bytes 262176 | tf_op jit(solution)/shard_map/ppermute | solution.py:14
  345.2 11.2 collective-permute-done.5
  362.1 6.3 fusion.65
  376.3 3.1 collective-permute-start.14
  403.8 4.9 fusion.58
  523.3 4.2 copy.223
  530.5 3.3 fusion.66
  546.5 276.8 %all-reduce.9.cloned.1.call-done = (f32[3456,128]{1,0:T(8,128)}, f32[3456,128]{1,0:T(8,128)}) async-done(((f32[3456,128]{1,0:T(8,128)}, f32[3456,128]{1,0:T(8,128)}), (f32[3456,128]{1,0:T(8,128)}, f32[3456,128]{1,0:T(8,128)})) %all-reduce.9.cloned.1.call-update) | async-done | bytes 3538960 | tf_op jit(solution)/shard_map/psum | solution.py:137
  840.6 4.7 copy.274
  845.4 4.0 fusion.5
  852.1 276.0 %all-reduce.11.cloned.1.call-done = (f32[3456,128]{1,0:T(8,128)}, f32[3456,128]{1,0:T(8,128)}) async-done(((f32[3456,128]{1,0:T(8,128)}, f32[3456,128]{1,0:T(8,128)}), (f32[3456,128]{1,0:T(8,128)}, f32[3456,128]{1,0:T(8,128)})) %all-reduce.11.cloned.1.call-update) | async-done | bytes 3538960 | tf_op jit(solution)/shard_map/psum | solution.py:137
  1128.1 2.9 broadcast_multiply_fusion.1
  (736 shorter events, 432.1 us)
Async XLA Ops:
  7.2 816.2 %all-reduce.9.cloned.1.call-start = ((), (), s32[]{:S(2)}) async-start(), calls=%async_computation | async-start | bytes 7077888 | tf_op jit(solution)/shard_map/psum | solution.py:137
  13.2 39.2 %collective-permute-start = (bf16[2,8,8,8,128]{4,3,2,1,0:T(8,128)(2,1)}, bf16[2,8,8,8,128]{4,3,2,1,0:T(8,128)(2,1)S(1)}, u32[]{:S(2)}, u32[]{:S(2)}) collective-permute-start(bf16[2,8,8,8,128]{4,3,2,1,0:T(8,128)(2,1)} %gather_fusion), channel_id=1, source_target_pairs={{0,1},{1,2},{2,3},{3,4},{4,5},{5,6},{6,7},{8,9},{9,10},{10,11},{11... | collective-permute-start | bytes 786440 | tf_op jit(solution)/shard_map/ppermute | solution.py:14
  23.6 28.8 %collective-permute-start.1 = (bf16[2,8,8,8,128]{4,3,2,1,0:T(8,128)(2,1)}, bf16[2,8,8,8,128]{4,3,2,1,0:T(8,128)(2,1)S(1)}, u32[]{:S(2)}, u32[]{:S(2)}) collective-permute-start(bf16[2,8,8,8,128]{4,3,2,1,0:T(8,128)(2,1)} %gather_fusion.1), channel_id=1, source_target_pairs={{1,0},{2,1},{3,2},{4,3},{5,4},{6,5},{7,6},{9,8},{10,9},{11,10},{12... | collective-permute-start | bytes 786440 | tf_op jit(solution)/shard_map/ppermute | solution.py:14
  26.8 34.0 %collective-permute-start.8 = (bf16[2,8,8,8,128]{4,3,2,1,0:T(8,128)(2,1)}, bf16[2,8,8,8,128]{4,3,2,1,0:T(8,128)(2,1)S(1)}, u32[]{:S(2)}, u32[]{:S(2)}) collective-permute-start(bf16[2,8,8,8,128]{4,3,2,1,0:T(8,128)(2,1)} %gather_fusion.62), channel_id=1, source_target_pairs={{0,1},{1,2},{2,3},{3,4},{4,5},{5,6},{6,7},{8,9},{9,10},{10,11},{11... | collective-permute-start | bytes 786440 | tf_op jit(solution)/shard_map/ppermute | solution.py:14
  35.9 34.3 %collective-permute-start.9 = (bf16[2,8,8,8,128]{4,3,2,1,0:T(8,128)(2,1)}, bf16[2,8,8,8,128]{4,3,2,1,0:T(8,128)(2,1)S(1)}, u32[]{:S(2)}, u32[]{:S(2)}) collective-permute-start(bf16[2,8,8,8,128]{4,3,2,1,0:T(8,128)(2,1)} %gather_fusion.63), channel_id=1, source_target_pairs={{1,0},{2,1},{3,2},{4,3},{5,4},{6,5},{7,6},{9,8},{10,9},{11,10},{12... | collective-permute-start | bytes 786440 | tf_op jit(solution)/shard_map/ppermute | solution.py:14
  72.5 18.1 %collective-permute-start.2 = (bf16[6,8,8,8,128]{4,3,2,1,0:T(8,128)(2,1)}, bf16[6,8,8,8,128]{4,3,2,1,0:T(8,128)(2,1)}, u32[]{:S(2)}, u32[]{:S(2)}) collective-permute-start(bf16[6,8,8,8,128]{4,3,2,1,0:T(8,128)(2,1)} %gather_fusion.2), channel_id=1, source_target_pairs={{0,8},{8,16},{16,24},{24,32},{32,40},{40,48},{48,56},{56,64},{64,7... | collective-permute-start | bytes 2359304 | tf_op jit(solution)/shard_map/ppermute | solution.py:14
  76.3 16.4 %collective-permute-start.3 = (bf16[6,8,8,8,128]{4,3,2,1,0:T(8,128)(2,1)}, bf16[6,8,8,8,128]{4,3,2,1,0:T(8,128)(2,1)S(1)}, u32[]{:S(2)}, u32[]{:S(2)}) collective-permute-start(bf16[6,8,8,8,128]{4,3,2,1,0:T(8,128)(2,1)} %gather_fusion.3), channel_id=1, source_target_pairs={{8,0},{16,8},{24,16},{32,24},{40,32},{48,40},{56,48},{64,56},{72,6... | collective-permute-start | bytes 2359304 | tf_op jit(solution)/shard_map/ppermute | solution.py:14
  82.2 21.7 %collective-permute-start.10 = (bf16[6,8,8,8,128]{4,3,2,1,0:T(8,128)(2,1)}, bf16[6,8,8,8,128]{4,3,2,1,0:T(8,128)(2,1)S(1)}, u32[]{:S(2)}, u32[]{:S(2)}) collective-permute-start(bf16[6,8,8,8,128]{4,3,2,1,0:T(8,128)(2,1)} %gather_fusion.64), channel_id=1, source_target_pairs={{0,8},{8,16},{16,24},{24,32},{32,40},{40,48},{48,56},{56,64},{64,7... | collective-permute-start | bytes 2359304 | tf_op jit(solution)/shard_map/ppermute | solution.py:14
  86.2 22.1 %collective-permute-start.11 = (bf16[6,8,8,8,128]{4,3,2,1,0:T(8,128)(2,1)}, bf16[6,8,8,8,128]{4,3,2,1,0:T(8,128)(2,1)S(1)}, u32[]{:S(2)}, u32[]{:S(2)}) collective-permute-start(bf16[6,8,8,8,128]{4,3,2,1,0:T(8,128)(2,1)} %gather_fusion.65), channel_id=1, source_target_pairs={{8,0},{16,8},{24,16},{32,24},{40,32},{48,40},{56,48},{64,56},{72,6... | collective-permute-start | bytes 2359304 | tf_op jit(solution)/shard_map/ppermute | solution.py:14
  300.8 24.1 %collective-permute-start.12 = (bf16[2,8,8,8,128]{4,3,2,1,0:T(8,128)(2,1)}, bf16[2,8,8,8,128]{4,3,2,1,0:T(8,128)(2,1)S(1)}, u32[]{:S(2)}, u32[]{:S(2)}) collective-permute-start(bf16[2,8,8,8,128]{4,3,2,1,0:T(8,128)(2,1)} %gather_fusion.93), channel_id=1, source_target_pairs={{0,1},{1,2},{2,3},{3,4},{4,5},{5,6},{6,7},{8,9},{9,10},{10,11},{11... | collective-permute-start | bytes 786440 | tf_op jit(solution)/shard_map/ppermute | solution.py:14
  307.4 37.7 %collective-permute-start.13 = (bf16[2,8,8,8,128]{4,3,2,1,0:T(8,128)(2,1)}, bf16[2,8,8,8,128]{4,3,2,1,0:T(8,128)(2,1)S(1)}, u32[]{:S(2)}, u32[]{:S(2)}) collective-permute-start(bf16[2,8,8,8,128]{4,3,2,1,0:T(8,128)(2,1)} %gather_fusion.94), channel_id=1, source_target_pairs={{1,0},{2,1},{3,2},{4,3},{5,4},{6,5},{7,6},{9,8},{10,9},{11,10},{12... | collective-permute-start | bytes 786440 | tf_op jit(solution)/shard_map/ppermute | solution.py:14
  311.5 33.7 %collective-permute-start.4 = (bf16[2,8,8,8,128]{4,3,2,1,0:T(8,128)(2,1)}, bf16[2,8,8,8,128]{4,3,2,1,0:T(8,128)(2,1)S(1)}, u32[]{:S(2)}, u32[]{:S(2)}) collective-permute-start(bf16[2,8,8,8,128]{4,3,2,1,0:T(8,128)(2,1)} %gather_fusion.31), channel_id=1, source_target_pairs={{0,1},{1,2},{2,3},{3,4},{4,5},{5,6},{6,7},{8,9},{9,10},{10,11},{11... | collective-permute-start | bytes 786440 | tf_op jit(solution)/shard_map/ppermute | solution.py:14
  317.1 39.3 %collective-permute-start.5 = (bf16[2,8,8,8,128]{4,3,2,1,0:T(8,128)(2,1)}, bf16[2,8,8,8,128]{4,3,2,1,0:T(8,128)(2,1)}, u32[]{:S(2)}, u32[]{:S(2)}) collective-permute-start(bf16[2,8,8,8,128]{4,3,2,1,0:T(8,128)(2,1)} %gather_fusion.32), channel_id=1, source_target_pairs={{1,0},{2,1},{3,2},{4,3},{5,4},{6,5},{7,6},{9,8},{10,9},{11,10},{12... | collective-permute-start | bytes 786440 | tf_op jit(solution)/shard_map/ppermute | solution.py:14
  359.3 25.4 %collective-permute-start.6 = (bf16[6,8,8,8,128]{4,3,2,1,0:T(8,128)(2,1)}, bf16[6,8,8,8,128]{4,3,2,1,0:T(8,128)(2,1)}, u32[]{:S(2)}, u32[]{:S(2)}) collective-permute-start(bf16[6,8,8,8,128]{4,3,2,1,0:T(8,128)(2,1)} %gather_fusion.33), channel_id=1, source_target_pairs={{0,8},{8,16},{16,24},{24,32},{32,40},{40,48},{48,56},{56,64},{64,7... | collective-permute-start | bytes 2359304 | tf_op jit(solution)/shard_map/ppermute | solution.py:14
  370.1 16.7 %collective-permute-start.7 = (bf16[6,8,8,8,128]{4,3,2,1,0:T(8,128)(2,1)}, bf16[6,8,8,8,128]{4,3,2,1,0:T(8,128)(2,1)}, u32[]{:S(2)}, u32[]{:S(2)}) collective-permute-start(bf16[6,8,8,8,128]{4,3,2,1,0:T(8,128)(2,1)} %gather_fusion.34), channel_id=1, source_target_pairs={{8,0},{16,8},{24,16},{32,24},{40,32},{48,40},{56,48},{64,56},{72,6... | collective-permute-start | bytes 2359304 | tf_op jit(solution)/shard_map/ppermute | solution.py:14
  376.3 23.0 %collective-permute-start.14 = (bf16[6,8,8,8,128]{4,3,2,1,0:T(8,128)(2,1)}, bf16[6,8,8,8,128]{4,3,2,1,0:T(8,128)(2,1)S(1)}, u32[]{:S(2)}, u32[]{:S(2)}) collective-permute-start(bf16[6,8,8,8,128]{4,3,2,1,0:T(8,128)(2,1)} %gather_fusion.95), channel_id=1, source_target_pairs={{0,8},{8,16},{16,24},{24,32},{32,40},{40,48},{48,56},{56,64},{64,7... | collective-permute-start | bytes 2359304 | tf_op jit(solution)/shard_map/ppermute | solution.py:14
  379.4 29.3 %collective-permute-start.15 = (bf16[6,8,8,8,128]{4,3,2,1,0:T(8,128)(2,1)}, bf16[6,8,8,8,128]{4,3,2,1,0:T(8,128)(2,1)}, u32[]{:S(2)}, u32[]{:S(2)}) collective-permute-start(bf16[6,8,8,8,128]{4,3,2,1,0:T(8,128)(2,1)} %gather_fusion.96), channel_id=1, source_target_pairs={{8,0},{16,8},{24,16},{32,24},{40,32},{48,40},{56,48},{64,56},{72,6... | collective-permute-start | bytes 2359304 | tf_op jit(solution)/shard_map/ppermute | solution.py:14
  533.8 594.4 %all-reduce.11.cloned.1.call-start = ((), (), s32[]{:S(2)}) async-start(), calls=%async_computation.1 | async-start | bytes 7077888 | tf_op jit(solution)/shard_map/psum | solution.py:137
  544.9 279.9 %copy-start.52 = (bf16[19,1,1,1,128]{4,3,2,1,0:T(2,128)(2,1)S(1)}, bf16[19,1,1,1,128]{4,3,2,1,0:T(2,128)(2,1)}, u32[]{:S(2)}) copy-start(bf16[19,1,1,1,128]{4,3,2,1,0:T(2,128)(2,1)} %get-tuple-element.11) | copy-start | bytes 14596
  544.9 280.7 %copy-start.51 = (bf16[19,1,1,1,128]{4,3,2,1,0:T(2,128)(2,1)S(1)}, bf16[19,1,1,1,128]{4,3,2,1,0:T(2,128)(2,1)}, u32[]{:S(2)}) copy-start(bf16[19,1,1,1,128]{4,3,2,1,0:T(2,128)(2,1)} %get-tuple-element.12) | copy-start | bytes 14596
  544.9 281.4 %copy-start.50 = (bf16[19,1,1,1,128]{4,3,2,1,0:T(2,128)(2,1)S(1)}, bf16[19,1,1,1,128]{4,3,2,1,0:T(2,128)(2,1)}, u32[]{:S(2)}) copy-start(bf16[19,1,1,1,128]{4,3,2,1,0:T(2,128)(2,1)} %get-tuple-element.13) | copy-start | bytes 14596
  545.7 284.2 %copy-start.34 = (bf16[19,1,8,1,128]{4,3,2,1,0:T(2,128)(2,1)S(1)}, bf16[19,1,8,1,128]{4,3,2,1,0:T(2,128)(2,1)}, u32[]{:S(2)}) copy-start(bf16[19,1,8,1,128]{4,3,2,1,0:T(2,128)(2,1)} %get-tuple-element.22) | copy-start | bytes 116740
  545.7 284.9 %copy-start.33 = (bf16[19,1,8,1,128]{4,3,2,1,0:T(2,128)(2,1)S(1)}, bf16[19,1,8,1,128]{4,3,2,1,0:T(2,128)(2,1)}, u32[]{:S(2)}) copy-start(bf16[19,1,8,1,128]{4,3,2,1,0:T(2,128)(2,1)} %get-tuple-element.23) | copy-start | bytes 116740
  545.7 287.3 %copy-start.23 = (bf16[2,8,1,10,128]{4,3,2,1,0:T(8,128)(2,1)S(1)}, bf16[2,8,1,10,128]{4,3,2,1,0:T(8,128)(2,1)}, u32[]{:S(2)}) copy-start(bf16[2,8,1,10,128]{4,3,2,1,0:T(8,128)(2,1)} %copy-done.22) | copy-start | bytes 122884
  (86 other events, 1344.9 us)
Sparse Core Ops, SparseCore 0:
  533.9 289.4 all-reduce.8
  826.3 301.7 all-reduce.10
